TPU v7x, 32 devices: a whole 2x2x4 slice. The times are simulated.
32 devices in a mesh: row: 4 (over z), col: 8 (over y, x, core).
Axes of the slice: x: 2, y: 2, z: 4, core: 2. Of those that a mesh axis runs over, the one named last changes fastest.
Arguments:
- factor: bfloat16 [16384, 16384], P('row', 'col'), may hold values from -1 to 7, as said below
- old_basis: bfloat16 [16384, 2048], P(('col', 'row')), may hold values from -9 to 9, as said below
- first_moment: float32 [16384, 2048], P(('col', 'row')), may hold values from -1.8 to 1.8
Outputs:
- new_basis: bfloat16 [16384, 2048], P(('col', 'row'))
- rotated_moment: float32 [16384, 2048], P(('col', 'row'))
Inputs may be any that keep to these rules, and one draw needn't show every extreme that they name: factor equals its transpose and is positive definite. old_basis has full column rank.
All inputs are finite; a program needn't handle non-finite values.
Results may differ from a plain program's by a relative error of at most 0.0053.
Values may be sent and summed in bfloat16 or wider, within the bound.
No kernel may reach another device: no remote copies, remote signals or barrier semaphores. Data moves between devices by JAX's collectives and lax.ppermute only.
A program may use at most 192 MiB of HBM per device.

v0:
```python
import jax
import jax.numpy as jnp
from jax import lax
from jax.sharding import PartitionSpec as P

M = 16384


def blocked_cholesky(gram_matrix):
    width = gram_matrix.shape[0]
    step_width = min(512, width)
    steps_total = width // step_width
    trailing = gram_matrix
    pieces = []
    inverses = []
    for position in range(steps_total):
        head = trailing[:step_width, :step_width]
        diag_factor = jnp.linalg.cholesky(head)
        inverse = jax.scipy.linalg.solve_triangular(
            diag_factor, jnp.eye(step_width, dtype=jnp.float32), lower=True
        )
        below = jnp.dot(
            trailing[step_width:, :step_width], inverse.T, precision=lax.Precision.HIGHEST
        )
        above = jnp.zeros((position * step_width, step_width), jnp.float32)
        pieces.append(jnp.concatenate([above, diag_factor, below], 0))
        inverses.append(inverse)
        trailing = trailing[step_width:, step_width:] - jnp.dot(
            below, below.T, precision=lax.Precision.HIGHEST
        )
    return (jnp.concatenate(pieces, 1), inverses, step_width)


def blocked_solve(lower_factor, inverses, step_width, rhs_matrix):
    solved = []
    for position in range(len(inverses)):
        begin = position * step_width
        current = rhs_matrix[:, begin : begin + step_width]
        if position > 0:
            earlier = jnp.concatenate(solved, 1)
            coupling = lower_factor[begin : begin + step_width, :begin]
            current = current - jnp.dot(earlier, coupling.T, precision=lax.Precision.HIGHEST)
        solved.append(jnp.dot(current, inverses[position].T, precision=lax.Precision.HIGHEST))
    return jnp.concatenate(solved, 1)


def body(factor, old_basis, first_moment):
    grid_rows = lax.axis_size("row")
    grid_columns = lax.axis_size("col")
    tile_rows, tile_columns = factor.shape
    slab_rows, panel_width = old_basis.shape
    groups = grid_columns // grid_rows
    column_panel = lax.all_gather(old_basis, "row", axis=0, tiled=True)
    sub_rows = slab_rows // grid_columns
    arranged = factor.reshape(groups, grid_rows, grid_columns, sub_rows, tile_columns)
    stripe = arranged
    stripe = jnp.transpose(stripe, (2, 1, 0, 3, 4)).reshape(
        lax.axis_size("col") * slab_rows, tile_columns
    )
    summed = lax.psum_scatter(
        jnp.dot(stripe, column_panel, preferred_element_type=jnp.float32),
        "col",
        scatter_dimension=0,
        tiled=True,
    )
    relayed = summed.astype(jnp.bfloat16).reshape(grid_rows, groups, sub_rows, panel_width)
    relayed = lax.all_to_all(relayed, "row", split_axis=0, concat_axis=0, tiled=True)
    relayed = relayed.reshape(grid_columns, sub_rows, panel_width)
    relayed = lax.all_to_all(relayed, "col", split_axis=0, concat_axis=0, tiled=True)
    product = relayed.reshape(slab_rows, panel_width)
    gram_part = lax.dot_general(
        product, product, (((0,), (0,)), ((), ())), preferred_element_type=jnp.float32
    )
    gram_part = gram_part * (1.0 / M)
    gram_matrix = lax.psum(gram_part, ("row", "col"))
    lower_factor, inverses, step_width = blocked_cholesky(gram_matrix)
    solved = blocked_solve(lower_factor, inverses, step_width, product.astype(jnp.float32))
    new_basis = solved.astype(jnp.bfloat16)
    rotated_moment = jnp.dot(first_moment, lower_factor, precision=lax.Precision.HIGHEST)
    return (new_basis, rotated_moment)


def solution(mesh):
    placed = (P("row", "col"), P(("col", "row"), None), P(("col", "row"), None))
    return jax.shard_map(
        body,
        mesh=mesh,
        in_specs=placed,
        out_specs=(P(("col", "row"), None), P(("col", "row"), None)),
        check_vma=False,
    )
```

profile of v0, /device:TPU:4, one launch (start us, length us, event | category | flops | bytes accessed | tf_op | source)
XLA Modules:
  0.0 1600.5 jit_solution(15312457744226294278)
XLA Ops:
  7.9 14.5 copy.31
  22.4 138.0 %all-gather.2.cloned.1.call-done = bf16[2048,2048]{1,0:T(8,128)(2,1)} async-done(((bf16[512,2048]{1,0:T(8,128)(2,1)}), bf16[2048,2048]{1,0:T(8,128)(2,1)}) %all-gather.2.cloned.1.call-update) | async-done | bytes 8388624 | tf_op jit(solution)/shard_map/all_gather | solution.py:53
  160.4 43.1 %fusion.205 = f32[4096,2048]{1,0:T(8,128)} fusion(bf16[4096,2048]{1,0:T(8,128)(2,1)} %bitcast.216, bf16[2048,2048]{1,0:T(8,128)(2,1)} %all-gather.2.cloned.1.call-done), kind=kOutput, calls=%fused_computation.352 | convolution fusion | flops 34359738368 | bytes 58720256 | tf_op jit(solution)/shard_map/dot_general | solution.py:61
  203.6 203.5 %reduce-scatter.2.cloned.1.call-done = f32[512,2048]{1,0:T(8,128)} async-done(((f32[4096,2048]{1,0:T(8,128)}), f32[512,2048]{1,0:T(8,128)}) %reduce-scatter.2.cloned.1.call-update) | async-done | bytes 4194320 | tf_op jit(solution)/shard_map/reduce_scatter | solution.py:60
  409.6 52.6 %all_to_all.10 = bf16[4,2,64,2048]{3,2,1,0:T(8,128)(2,1)S(1)} all-to-all(bf16[4,2,64,2048]{3,2,1,0:T(8,128)(2,1)S(1)} %bitcast.218), channel_id=1, replica_groups=mesh['row'=4,'col'=8] {'row'}, dimensions={0} | all-to-all | bytes 4194304 | tf_op jit(solution)/shard_map/all_to_all | solution.py:67
  462.2 28.3 %all_to_all.11 = bf16[8,64,2048]{2,1,0:T(8,128)(2,1)S(1)} all-to-all(bf16[8,64,2048]{2,1,0:T(8,128)(2,1)S(1)} %bitcast.219), channel_id=1, replica_groups=mesh['row'=4,'col'=8] {'col'}, dimensions={0} | all-to-all | bytes 4194304 | tf_op jit(solution)/shard_map/all_to_all | solution.py:69
  501.6 273.5 %all-reduce.4.cloned.1.call-done = f32[2048,2048]{0,1:T(8,128)} async-done(((f32[2048,2048]{0,1:T(8,128)}), f32[2048,2048]{0,1:T(8,128)}) %all-reduce.4.cloned.1.call-update) | async-done | bytes 16777232 | tf_op jit(solution)/shard_map/psum | solution.py:75
  778.2 11.7 cholesky.462
  800.6 11.7 cholesky.481
  823.2 11.7 cholesky.502
  846.0 11.8 cholesky.519
  870.7 39.3 %custom-call.38 = f32[4,128,128]{1,2,0:T(8,128)S(1)} custom-call(f32[4,128,128]{2,1,0:T(8,128)S(1)} %get-tuple-element.30), custom_call_target="InvertDiagBlocksLowerTriangular" | custom-call | tf_op jit(solution)/shard_map/jit(_solve_triangular)/triangular_solve | solution.py:19
  914.0 12.1 fusion.28
  926.1 19.1 %slice_subtract_fusion = f32[1536,1536]{0,1:T(8,128)S(1)} fusion(f32[2048,2048]{0,1:T(8,128)} %all-reduce.4.cloned.1.call-done, f32[1536,512]{1,0:T(8,128)S(1)} %fusion.28), kind=kOutput, calls=%fused_computation.28 | convolution fusion | flops 14497873920 | bytes 25165824 | tf_op jit(solution)/shard_map/dot_general | solution.py:28
  955.2 11.7 cholesky.534
  981.0 11.7 cholesky.553
  1007.1 11.7 cholesky.574
  1032.2 11.7 cholesky.591
  1062.7 39.9 %custom-call.42 = f32[4,128,128]{1,2,0:T(8,128)} custom-call(f32[4,128,128]{2,1,0:T(8,128)S(1)} %get-tuple-element.31), custom_call_target="InvertDiagBlocksLowerTriangular" | custom-call | tf_op jit(solution)/shard_map/jit(_solve_triangular)/triangular_solve | solution.py:19
  1138.3 11.7 cholesky.606
  1164.8 11.7 cholesky.625
  1192.6 13.2 cholesky.646
  1222.2 11.7 cholesky.663
  1241.2 13.3 while.10
  1254.6 40.7 %custom-call.46 = f32[4,128,128]{1,2,0:T(8,128)} custom-call(f32[4,128,128]{2,1,0:T(8,128)} %get-tuple-element.32), custom_call_target="InvertDiagBlocksLowerTriangular" | custom-call | tf_op jit(solution)/shard_map/jit(_solve_triangular)/triangular_solve | solution.py:19
  1318.2 11.9 cholesky.678
  1347.8 11.7 cholesky.697
  1376.9 13.6 cholesky.718
  1407.0 11.7 cholesky.735
  1428.1 65.0 %fusion.19 = f32[512,2048]{0,1:T(8,128)} fusion(f32[512,2048]{1,0:T(8,128)} %param.8, f32[512,512]{1,0:T(8,128)} %get-tuple-element.73, f32[512,512]{1,0:T(8,128)} %copy-done.8, f32[512,512]{1,0:T(8,128)} %get-tuple-element.75, f32[1024,512]{1,0:T(8,128)} %broadcast_in_dim.9, f32[1024,512]{1,0:T(8,128)} %copy-done.1, f32[512,512]{1,0:T(8,128)} %get-tuple-element.77, ...), kind=kOutput, calls=%fused_computation.32 | convolution fusion | flops 25811746816 | bytes 22020096 | tf_op jit(solution)/shard_map/dot_general | solution.py:79
  1499.1 14.1 while.11
  1513.2 40.7 %custom-call.50 = f32[4,128,128]{1,2,0:T(8,128)} custom-call(f32[4,128,128]{2,1,0:T(8,128)} %get-tuple-element.33), custom_call_target="InvertDiagBlocksLowerTriangular" | custom-call | tf_op jit(solution)/shard_map/jit(_solve_triangular)/triangular_solve | solution.py:19
  (298 shorter events, 393.0 us)
Async XLA Ops:
  7.2 153.3 %all-gather.2.cloned.1.call-start = ((), (), s32[]{:S(2)}) async-start(), calls=%async_computation.3 | async-start | bytes 10485760 | tf_op jit(solution)/shard_map/all_gather | solution.py:53
  7.9 399.2 %reduce-scatter.2.cloned.1.call-start = ((), (), s32[]{:S(2)}) async-start(), calls=%async_computation.4 | async-start | bytes 37748736 | tf_op jit(solution)/shard_map/reduce_scatter | solution.py:60
  203.6 571.5 %all-reduce.4.cloned.1.call-start = ((), (), s32[]{:S(2)}) async-start(), calls=%async_computation.5 | async-start | bytes 33554432 | tf_op jit(solution)/shard_map/psum | solution.py:75
  490.5 8.4 copy-start.7
  498.9 413.3 %copy-start.3 = (f32[512,512]{1,0:T(8,128)}, f32[512,512]{1,0:T(8,128)S(1)}, u32[]{:S(2)}) copy-start(f32[512,512]{1,0:T(8,128)S(1)} %fusion.65) | copy-start | bytes 3145732
  910.5 2.8 copy-start.10
  945.2 3.6 copy-start
  1102.7 5.6 copy-start.43
  1106.8 4.2 copy-start.14
  1120.0 9.7 copy-start.1
  1295.3 10.2 copy-start.5
  1296.9 12.2 copy-start.12
  1299.6 9.5 copy-start.18
  1302.4 3.1 copy-start.24
  1305.5 3.6 copy-start.36
  1553.9 5.6 copy-start.42
  1553.9 8.4 copy-start.11
  1553.9 8.4 copy-start.17
  1553.9 8.4 copy-start.23
  1553.9 8.4 copy-start.35
  1559.5 5.0 copy-start.6
  1562.3 5.7 copy-start.15
  1562.4 5.7 copy-start.21
  1562.4 5.7 copy-start.33
  1564.5 5.4 copy-start.2
  1564.5 5.4 copy-start.26
  1564.5 5.4 copy-start.27
  1564.6 5.4 copy-start.28
  1570.0 6.9 copy-start.13
  1570.0 6.9 copy-start.19
  1570.0 6.9 copy-start.25
  1570.0 6.9 copy-start.37
  (15 other events, 20.5 us)
Sparse Core Ops, SparseCore 0:
  9.6 150.8 all-gather.1
  203.7 203.3 reduce-scatter.1
  498.9 276.1 all-reduce.3
where the time goes:
time: 1610 us; the launch traced here: 1600 us
  waiting for transfers between devices  616 us (38%)
  other arithmetic  515 us (32%)
  matrix products  259 us (16%)
  local copies, waits for them, and re-layouts  104 us (6%)
  blocking collectives  80.9 us (5%)
  between operations  25.4 us (2%)
    another operation x59, other arithmetic, blocked_cholesky(): diag_factor = jnp.linalg.cholesky(head)  332 us
    psum x1, waiting for transfers between devices, body(): gram_matrix = lax.psum(gram_part, ('row', 'col'))  273 us
    reduce_scatter x1, waiting for transfers between devices, body(): lax.psum_scatter(jnp.dot(stripe, column_panel, preferred_element_type=jnp...  203 us
    another operation x9, other arithmetic, blocked_cholesky(): jax.scipy.linalg.solve_triangular(diag_factor, jnp.eye(step_width, dtype=...  170 us
    all_gather x1, waiting for transfers between devices, body(): column_panel = lax.all_gather(old_basis, 'row', axis=0, tiled=True)  138 us
    dot_general x1, matrix products, body(): jnp.dot(first_moment, lower_factor, precision=lax.Precision.HIGHEST)  65 us
    all_to_all x1, blocking collectives, body(): lax.all_to_all(relayed, 'row', split_axis=0, concat_axis=0, tiled=True)  52.6 us
    another operation x53, local copies, waits for them, and re-layouts, blocked_cholesky(): jax.scipy.linalg.solve_triangular(diag_factor, jnp.eye(step_width, dtype=...  48 us
  transfers between devices with their start and end apart: 3, of which 3 were waited for; matrix products, arithmetic and copies ran while one was open for 1% of the time, Pallas kernels for 0%

commit v1 on v0

v1 whole, which is shorter than its diff:
```python
import functools

import jax
import jax.numpy as jnp
from jax import lax
from jax.experimental import pallas as pl
from jax.experimental.pallas import tpu as pltpu
from jax.sharding import PartitionSpec as P

F32 = jnp.float32
BF16 = jnp.bfloat16
LEAF = 128
GROUP = 8
STRIP = 4 * LEAF


def pieces(values):
    high = values.astype(BF16)
    rest = values - high.astype(F32)
    middle = rest.astype(BF16)
    low = (rest - middle.astype(F32)).astype(BF16)
    return high, middle, low


def left_form(values):
    high, middle, low = pieces(values)
    return jnp.concatenate([high, high, middle, high, low, middle], 1)


def right_form(values):
    high, middle, low = pieces(values)
    return jnp.concatenate([high, middle, high, low, high, middle], 1)


def times_transposed(left, right):
    return lax.dot_general(left, right, (((1,), (1,)), ((), ())), preferred_element_type=F32)


def full_times_transposed(left, right):
    return times_transposed(left_form(left), right_form(right))


def leaf_factor(block):
    size = block.shape[0]
    groups = size // GROUP
    shape = (GROUP, size)
    lane = lax.broadcasted_iota(jnp.int32, shape, 1)
    sub = lax.broadcasted_iota(jnp.int32, shape, 0)
    rows = [block[GROUP * g : GROUP * (g + 1), :] for g in range(groups)]
    upper, inverse = [], []
    for g in range(groups):
        first = GROUP * g
        inside = (lane >= first) & (lane < first + GROUP)
        columns = {
            h: [
                jnp.broadcast_to(rows[h][:, first + c : first + c + 1], shape)
                for c in range(GROUP)
            ]
            for h in range(g, groups)
        }
        rows[g] = jnp.where(inside, jnp.where(lane == sub + first, 1.0, 0.0), rows[g])
        for h in range(g + 1, groups):
            rows[h] = jnp.where(inside, 0.0, rows[h])
        scale = jnp.ones(shape, F32)
        for c in range(GROUP):
            pivot = jnp.broadcast_to(columns[g][c][c : c + 1, :], shape)
            root = lax.rsqrt(pivot)
            ratio = root * root
            scale = jnp.where(sub == c, root, scale)
            factors = {g: jnp.where(sub > c, columns[g][c] * ratio, 0.0)}
            for h in range(g + 1, groups):
                factors[h] = columns[h][c] * ratio
            for later in range(c + 1, GROUP):
                entry = jnp.broadcast_to(columns[g][later][c : c + 1, :], shape)
                for h in range(g, groups):
                    columns[h][later] = columns[h][later] - factors[h] * entry
            pivot_row = jnp.broadcast_to(rows[g][c : c + 1, :], shape)
            for h in range(g, groups):
                rows[h] = rows[h] - factors[h] * pivot_row
        top = rows[g]
        for c in range(GROUP):
            top = jnp.where(lane == first + c, columns[g][c], top)
        upper.append(jnp.where(lane >= sub + first, top * scale, 0.0))
        inverse.append(jnp.where(lane <= sub + first, rows[g] * scale, 0.0))
    return jnp.concatenate(upper, 0).T, jnp.concatenate(inverse, 0)


def panel_kernel(strip, groups, *refs):
    gram_refs = refs[: len(groups)]
    product_ref, moment_ref, basis_ref, rotated_ref = refs[len(groups) : len(groups) + 4]
    work, rest, left_panel, right_panel, arrivals = refs[len(groups) + 4 :]
    width = work.shape[0]
    strips = width // strip
    double = 2 * LEAF

    copies = []
    for group, gram_ref in zip(groups, gram_refs):
        begin = 0
        for s in group:
            length = (s + 1) * strip
            copies.append(
                pltpu.make_async_copy(
                    gram_ref.at[:, pl.ds(begin, length)],
                    work.at[pl.ds(s * strip, strip), pl.ds(0, length)],
                    arrivals.at[s],
                )
            )
            begin += length
    for copy in copies:
        copy.start()
    rest[...] = product_ref[...].astype(F32)
    for copy in copies:
        copy.wait()

    row_ids = lax.broadcasted_iota(jnp.int32, (strip, double), 0)

    def step(k, carry):
        here = pl.multiple_of(k * double, double)
        half = pl.multiple_of(here + LEAF, LEAF)
        below = here + double
        factor_a, inverse_a = leaf_factor(work[pl.ds(here, LEAF), pl.ds(here, LEAF)])
        side = full_times_transposed(work[pl.ds(half, LEAF), pl.ds(here, LEAF)], inverse_a)
        corner = work[pl.ds(half, LEAF), pl.ds(half, LEAF)] - full_times_transposed(side, side)
        factor_b, inverse_b = leaf_factor(corner)
        cross = full_times_transposed(side, inverse_a.T)
        inverse_side = -full_times_transposed(inverse_b, cross.T)
        work[pl.ds(here, LEAF), pl.ds(here, LEAF)] = factor_a
        work[pl.ds(half, LEAF), pl.ds(here, LEAF)] = side
        work[pl.ds(half, LEAF), pl.ds(half, LEAF)] = factor_b
        nothing = jnp.zeros((LEAF, LEAF), F32)
        inverse = jnp.concatenate(
            [
                jnp.concatenate([inverse_a, nothing], 1),
                jnp.concatenate([inverse_side, inverse_b], 1),
            ],
            0,
        )
        inverse_form = right_form(inverse)

        solved = times_transposed(left_form(rest[:, pl.ds(here, double)]), inverse_form)
        basis_ref[:, pl.ds(here, double)] = solved.astype(BF16)
        solved_form = left_form(solved)

        first_tile = below // strip

        def one_panel(tile, carry):
            at = pl.multiple_of(tile * strip, strip)
            old = work[pl.ds(at, strip), pl.ds(here, double)]
            new = times_transposed(left_form(old), inverse_form)
            live = row_ids + at >= below
            work[pl.ds(at, strip), pl.ds(here, double)] = jnp.where(live, new, old)
            new = jnp.where(live, new, 0.0)
            left_panel[pl.ds(at, strip), :] = left_form(new)
            right_panel[pl.ds(at, strip), :] = right_form(new)
            return carry

        lax.fori_loop(first_tile, strips, one_panel, 0)

        def one_strip(column, carry):
            at = pl.multiple_of(column * strip, strip)
            right = right_panel[pl.ds(at, strip), :]
            rest[:, pl.ds(at, strip)] -= times_transposed(solved_form, right)

            def one_tile(tile, carry):
                top = pl.multiple_of(tile * strip, strip)
                work[pl.ds(top, strip), pl.ds(at, strip)] -= times_transposed(
                    left_panel[pl.ds(top, strip), :], right_panel[pl.ds(at, strip), :]
                )
                return carry

            return lax.fori_loop(column, strips, one_tile, carry)

        lax.fori_loop(first_tile, strips, one_strip, 0)
        return carry

    lax.fori_loop(0, width // double, step, 0)

    tile_rows = lax.broadcasted_iota(jnp.int32, (strip, strip), 0)
    tile_columns = lax.broadcasted_iota(jnp.int32, (strip, strip), 1)

    def rotate_strip(column, carry):
        at = pl.multiple_of(column * strip, strip)
        rotated_ref[:, pl.ds(at, strip)] = jnp.zeros((rotated_ref.shape[0], strip), F32)

        def rotate_tile(tile, carry):
            top = pl.multiple_of(tile * strip, strip)
            lower = work[pl.ds(top, strip), pl.ds(at, strip)]
            lower = jnp.where(tile_rows + top >= tile_columns + at, lower, 0.0)
            lower_high = lower.astype(BF16)
            lower_rest = (lower - lower_high.astype(F32)).astype(BF16)
            moment = moment_ref[:, pl.ds(top, strip)]
            moment_high = moment.astype(BF16)
            moment_rest = (moment - moment_high.astype(F32)).astype(BF16)
            rotated_ref[:, pl.ds(at, strip)] += jnp.dot(
                jnp.concatenate([moment_high, moment_high, moment_rest], 1),
                jnp.concatenate([lower_high, lower_rest, lower_high], 0),
                preferred_element_type=F32,
            )
            return carry

        return lax.fori_loop(column, strips, rotate_tile, carry)

    lax.fori_loop(0, strips, rotate_strip, 0)


def factor_and_apply(gram_groups, groups, product, moment, strip):
    slab, width = product.shape
    return pl.pallas_call(
        functools.partial(panel_kernel, strip, groups),
        out_shape=(
            jax.ShapeDtypeStruct((slab, width), BF16),
            jax.ShapeDtypeStruct((slab, width), F32),
        ),
        in_specs=[
            *[pl.BlockSpec(memory_space=pl.ANY) for _ in groups],
            pl.BlockSpec(memory_space=pltpu.VMEM),
            pl.BlockSpec(memory_space=pltpu.VMEM),
        ],
        out_specs=(
            pl.BlockSpec(memory_space=pltpu.VMEM),
            pl.BlockSpec(memory_space=pltpu.VMEM),
        ),
        scratch_shapes=[
            pltpu.VMEM((width, width), F32),
            pltpu.VMEM((slab, width), F32),
            pltpu.VMEM((width, 12 * LEAF), BF16),
            pltpu.VMEM((width, 12 * LEAF), BF16),
            pltpu.SemaphoreType.DMA((width // strip,)),
        ],
        compiler_params=pltpu.CompilerParams(vmem_limit_bytes=60 * 2**20),
        cost_estimate=pl.CostEstimate(
            flops=40 * 10**9, bytes_accessed=24 * 2**20, transcendentals=0
        ),
    )(*gram_groups, product, moment)


def bits_of(axis):
    size = lax.axis_size(axis)
    return [(axis, 1 << place) for place in range(size.bit_length() - 1)]


def side_of(dim):
    axis, bit = dim
    return (lax.axis_index(axis) // bit) % 2


def swap(values, dim):
    axis, bit = dim
    return lax.ppermute(values, axis, [(i, i ^ bit) for i in range(lax.axis_size(axis))])


def halve(values, dim, at):
    side = side_of(dim)
    size = values.shape[at] // 2
    kept = lax.dynamic_slice_in_dim(values, side * size, size, at)
    sent = lax.dynamic_slice_in_dim(values, (1 - side) * size, size, at)
    return kept + swap(sent, dim)


def double(values, dim):
    first = side_of(dim) == 0
    other = swap(values, dim)
    return jnp.concatenate([jnp.where(first, values, other), jnp.where(first, other, values)], 0)


def gather_rows(block):
    size = lax.axis_size("row")
    me = lax.axis_index("row")
    rows = block.shape[0]
    upward, downward = [block], [block]
    for step in range(1, size):
        upward.append(
            lax.ppermute(upward[-1], "row", [(i, i + 1) for i in range(step - 1, size - 1)])
        )
        downward.append(
            lax.ppermute(downward[-1], "row", [(i + 1, i) for i in range(size - step)])
        )
    panel = jnp.zeros((size * rows, block.shape[1]), block.dtype)
    for step in range(size):
        held = block
        if step > 0:
            held = jnp.where(me >= step, upward[step], downward[size - step])
        source = lax.rem(me - step + size, size)
        panel = lax.dynamic_update_slice_in_dim(panel, held, source * rows, 0)
    return panel


def scatter_columns(partial, slab_rows):
    dims = bits_of("col")
    count = len(dims)
    width = partial.shape[1]
    blocks = partial.reshape((2,) * count + (slab_rows, width))
    blocks = halve(blocks, dims[0], count - 1)
    blocks = blocks.reshape((2,) * (count - 1) + (slab_rows, width))
    others = dims[1:]
    finished = []
    for turn in range(2):
        piece = blocks[..., turn * (width // 2) : (turn + 1) * (width // 2)]
        order = list(range(count - 1))
        if turn == 1:
            order.reverse()
        for which in order:
            piece = halve(piece, others[which], count - 2 - which)
        finished.append(piece.reshape(slab_rows, width // 2))
    return jnp.concatenate(finished, 1)


def sum_gram(half, core, others):
    rows = half.shape[0] // 2
    finished = []
    for turn in range(2):
        piece = half[turn * rows : (turn + 1) * rows]
        order = list(others)
        if turn == 1:
            order[0], order[1] = order[1], order[0]
        for dim in order:
            piece = halve(piece, dim, 0)
        for dim in reversed(order):
            piece = double(piece, dim)
        finished.append(piece)
    return double(jnp.concatenate(finished, 0), core)


def body(factor, old_basis, first_moment):
    grid_rows = lax.axis_size("row")
    grid_columns = lax.axis_size("col")
    slab_rows, panel_width = old_basis.shape
    total_rows = slab_rows * grid_rows * grid_columns
    count = panel_width // STRIP
    core, *others = bits_of("col")
    others = others + bits_of("row")
    core_side = side_of(core)
    to_owner = [
        (slab, (slab % grid_rows) * grid_columns + slab // grid_rows)
        for slab in range(grid_rows * grid_columns)
    ]
    groups = [tuple(range(count - 2))] if count > 2 else []
    groups += [(s,) for s in range(max(count - 2, 0), count)]

    shared, owned, gram_groups = [], [], []
    for chunk in range(count):
        panel = gather_rows(old_basis[:, chunk * STRIP : (chunk + 1) * STRIP])
        partial = jnp.dot(factor, panel, preferred_element_type=F32)
        landed = scatter_columns(partial, slab_rows).astype(BF16)
        shared.append(jnp.concatenate([landed, swap(landed, core)], 0))
        owned.append(lax.ppermute(landed, ("row", "col"), to_owner))
        for group in groups:
            if group[-1] != chunk:
                continue
            parts = []
            for s in group:
                mine = lax.dynamic_slice_in_dim(
                    shared[s], core_side * (STRIP // 2), STRIP // 2, 1
                )
                for t in range(s + 1):
                    parts.append(
                        lax.dot_general(
                            mine, shared[t], (((0,), (0,)), ((), ())),
                            preferred_element_type=F32,
                        )
                    )
            half = jnp.concatenate(parts, 1) * (1.0 / total_rows)
            gram_groups.append(sum_gram(half, core, others))
    product = jnp.concatenate(owned, 1)
    return factor_and_apply(gram_groups, groups, product, first_moment, STRIP)


def solution(mesh):
    placed = (P("row", "col"), P(("col", "row"), None), P(("col", "row"), None))
    return jax.shard_map(
        body,
        mesh=mesh,
        in_specs=placed,
        out_specs=(P(("col", "row"), None), P(("col", "row"), None)),
        check_vma=False,
    )
```

time: 1610 us -> 851 us (0.53)
  other arithmetic: 515 us -> 48.6 us
  waiting for transfers between devices: 616 us -> 352 us
  matrix products: 259 us -> 64.4 us
  Pallas kernels: 0 us -> 156 us
  starting transfers between devices: 0.12 us -> 150 us
  blocking collectives: 80.9 us -> 0 us
  local copies, waits for them, and re-layouts: 104 us -> 68.1 us
  between operations: 25.4 us -> 2.51 us
    another operation x68 -> x0, other arithmetic: 503 us -> none  [the longest x59 332 us: blocked_cholesky(): diag_factor = jnp.linalg.cholesky(head)]
    ppermute x0 -> x103, waiting for transfers between devices: none -> 352 us  [the longest x75 261 us: swap(): lax.ppermute(values, axis, [(i, i ^ bit) for i in range(lax.axis_size(axi...]
    psum x1 -> x0, waiting for transfers between devices: 273 us -> none  [body(): gram_matrix = lax.psum(gram_part, ('row', 'col'))]
    reduce_scatter x1 -> x0, waiting for transfers between devices: 203 us -> none  [body(): lax.psum_scatter(jnp.dot(stripe, column_panel, preferred_element_type=jnp...]
    pallas_call x0 -> x1, Pallas kernels: none -> 156 us  [factor_and_apply(): pl.pallas_call(functools.partial(panel_kernel, strip, groups), out_shape=...]
    ppermute x0 -> x103, starting transfers between devices: none -> 150 us  [the longest x75 92.9 us: swap(): lax.ppermute(values, axis, [(i, i ^ bit) for i in range(lax.axis_size(axi...]
    all_gather x1 -> x0, waiting for transfers between devices: 138 us -> none  [body(): column_panel = lax.all_gather(old_basis, 'row', axis=0, tiled=True)]
    dot_general x16 -> x14, matrix products: 200 us -> 64.4 us  [the longest x4 59.7 us: body(): partial = jnp.dot(factor, panel, preferred_element_type=F32)]
  transfers between devices with their start and end apart: 3 -> 103, of which waited for: 3 -> 49; matrix products, arithmetic and copies ran while one was open for 1% -> 21% of each run, Pallas kernels for 0% -> 0%
where the time goes in v1:
time: 851 us; the launch traced here: 842 us
  waiting for transfers between devices  352 us (41%)
  Pallas kernels  156 us (18%)
  starting transfers between devices  150 us (18%)
  local copies, waits for them, and re-layouts  68.1 us (8%)
  matrix products  64.4 us (8%)
  other arithmetic  48.6 us (6%)
    ppermute x75, waiting for transfers between devices, swap(): lax.ppermute(values, axis, [(i, i ^ bit) for i in range(lax.axis_size(axi...  261 us
    pallas_call x1, Pallas kernels, factor_and_apply(): pl.pallas_call(functools.partial(panel_kernel, strip, groups), out_shape=...  156 us
    ppermute x75, starting transfers between devices, swap(): lax.ppermute(values, axis, [(i, i ^ bit) for i in range(lax.axis_size(axi...  92.9 us
    dot_general x4, matrix products, body(): partial = jnp.dot(factor, panel, preferred_element_type=F32)  59.7 us
    ppermute x12, waiting for transfers between devices, gather_rows(): lax.ppermute(downward[-1], 'row', [(i + 1, i) for i in range(size - step)])  47.6 us
    ppermute x4, waiting for transfers between devices, body(): owned.append(lax.ppermute(landed, ('row', 'col'), to_owner))  43.1 us
    dot_general x4, local copies, waits for them, and re-layouts, body(): partial = jnp.dot(factor, panel, preferred_element_type=F32)  36.3 us
    ppermute x12, starting transfers between devices, gather_rows(): lax.ppermute(upward[-1], 'row', [(i, i + 1) for i in range(step - 1, size...  30.8 us
  transfers between devices with their start and end apart: 103, of which 49 were waited for; matrix products, arithmetic and copies ran while one was open for 21% of the time, Pallas kernels for 0%

profile of v1, /device:TPU:4, one launch (start us, length us, event | category | flops | bytes accessed | tf_op | source)
XLA Modules:
  0.0 842.4 jit_solution(16578132956476953729)
XLA Ops:
  9.1 9.7 %collective-permute-done.71 = bf16[512,512]{1,0:T(8,128)(2,1)S(1)} collective-permute-done((bf16[512,512]{1,0:T(8,128)(2,1)S(1)}, bf16[512,512]{1,0:T(8,128)(2,1)S(1)}, u32[]{:S(2)}, u32[]{:S(2)}) %collective-permute-start.71) | collective-permute-done | bytes 524320 | tf_op jit(solution)/shard_map/ppermute | solution.py:276
  22.9 9.6 %collective-permute-start.41 = (bf16[512,512]{1,0:T(8,128)(2,1)}, bf16[512,512]{1,0:T(8,128)(2,1)}, u32[]{:S(2)}, u32[]{:S(2)}) collective-permute-start(bf16[512,512]{1,0:T(8,128)(2,1)} %get-tuple-element.22), channel_id=1, source_target_pairs={{0,8},{8,16},{16,24},{1,9},{9,17},{17,25},{2,10},{10,18},{18,26},{... | collective-permute-start | bytes 1572872 | tf_op jit(solution)/shard_map/ppermute | solution.py:273
  43.3 24.0 %collective-permute-done.73 = bf16[512,512]{1,0:T(8,128)(2,1)} collective-permute-done((bf16[512,512]{1,0:T(8,128)(2,1)}, bf16[512,512]{1,0:T(8,128)(2,1)}, u32[]{:S(2)}, u32[]{:S(2)}) %collective-permute-start.73) | collective-permute-done | bytes 524320 | tf_op jit(solution)/shard_map/ppermute | solution.py:276
  90.8 8.1 collective-permute-done.43
  100.9 15.2 %convolution_bitcast_fusion = f32[4096,512]{0,1:T(8,128)} fusion(bf16[2048,512]{1,0:T(8,128)(2,1)} %select_dynamic-update-slice_fusion, bf16[4096,2048]{1,0:T(8,128)(2,1)} %param.3), kind=kOutput, calls=%fused_computation | convolution fusion | flops 8589934592 | bytes 27262976 | tf_op jit(solution)/shard_map/dot_general | solution.py:343
  116.0 9.0 %copy.14 = f32[4096,512]{1,0:T(8,128)} copy(f32[4096,512]{0,1:T(8,128)} %convolution_bitcast_fusion) | data formatting | bytes 16777216 | tf_op jit(solution)/shard_map/dot_general | solution.py:343
  142.5 15.1 %convolution_bitcast_fusion.1 = f32[4096,512]{0,1:T(8,128)} fusion(bf16[2048,512]{1,0:T(8,128)(2,1)} %select_dynamic-update-slice_fusion.3, bf16[4096,2048]{1,0:T(8,128)(2,1)} %param.3), kind=kOutput, calls=%fused_computation.1 | convolution fusion | flops 8589934592 | bytes 27262976 | tf_op jit(solution)/shard_map/dot_general | solution.py:343
  157.6 9.1 %copy.11 = f32[4096,512]{1,0:T(8,128)} copy(f32[4096,512]{0,1:T(8,128)} %convolution_bitcast_fusion.1) | data formatting | bytes 16777216 | tf_op jit(solution)/shard_map/dot_general | solution.py:343
  174.5 14.8 %convolution_bitcast_fusion.3 = f32[4096,512]{0,1:T(8,128)} fusion(bf16[2048,512]{1,0:T(8,128)(2,1)S(1)} %select_dynamic-update-slice_fusion.9, bf16[4096,2048]{1,0:T(8,128)(2,1)} %param.3), kind=kOutput, calls=%fused_computation.3 | convolution fusion | flops 8589934592 | bytes 27262976 | tf_op jit(solution)/shard_map/dot_general | solution.py:343
  189.3 9.2 %copy.5 = f32[4096,512]{1,0:T(8,128)} copy(f32[4096,512]{0,1:T(8,128)} %convolution_bitcast_fusion.3) | data formatting | bytes 16777216 | tf_op jit(solution)/shard_map/dot_general | solution.py:343
  204.8 14.7 %convolution_bitcast_fusion.2 = f32[4096,512]{0,1:T(8,128)} fusion(bf16[2048,512]{1,0:T(8,128)(2,1)S(1)} %select_dynamic-update-slice_fusion.6, bf16[4096,2048]{1,0:T(8,128)(2,1)} %param.3), kind=kOutput, calls=%fused_computation.2 | convolution fusion | flops 8589934592 | bytes 27262976 | tf_op jit(solution)/shard_map/dot_general | solution.py:343
  219.4 9.0 %copy.8 = f32[4096,512]{1,0:T(8,128)} copy(f32[4096,512]{0,1:T(8,128)} %convolution_bitcast_fusion.2) | data formatting | bytes 16777216 | tf_op jit(solution)/shard_map/dot_general | solution.py:343
  258.8 7.2 collective-permute-done.77
  268.1 20.4 %collective-permute-done.48 = f32[2,1,512,256]{3,2,1,0:T(8,128)} collective-permute-done((f32[2,1,512,256]{3,2,1,0:T(8,128)}, f32[2,1,512,256]{3,2,1,0:T(8,128)}, u32[]{:S(2)}, u32[]{:S(2)}) %collective-permute-start.48) | collective-permute-done | bytes 1048608 | tf_op jit(solution)/shard_map/ppermute | solution.py:249
  296.6 14.2 %collective-permute-done.7 = f32[2,1,512,256]{3,2,1,0:T(8,128)S(1)} collective-permute-done((f32[2,1,512,256]{3,2,1,0:T(8,128)S(1)}, f32[2,1,512,256]{3,2,1,0:T(8,128)S(1)}, u32[]{:S(2)}, u32[]{:S(2)}) %collective-permute-start.7) | collective-permute-done | bytes 1048608 | tf_op jit(solution)/shard_map/ppermute | solution.py:249
  313.3 20.1 %collective-permute-done.19 = f32[2,1,512,256]{3,2,1,0:T(8,128)S(1)} collective-permute-done((f32[2,1,512,256]{3,2,1,0:T(8,128)S(1)}, f32[2,1,512,256]{3,2,1,0:T(8,128)S(1)}, u32[]{:S(2)}, u32[]{:S(2)}) %collective-permute-start.19) | collective-permute-done | bytes 1048608 | tf_op jit(solution)/shard_map/ppermute | solution.py:249
  335.9 10.1 %collective-permute-done.78 = f32[1,1,512,256]{3,2,1,0:T(8,128)S(1)} collective-permute-done((f32[1,1,512,256]{3,2,1,0:T(8,128)S(1)}, f32[1,1,512,256]{3,2,1,0:T(8,128)S(1)}, u32[]{:S(2)}, u32[]{:S(2)}) %collective-permute-start.78) | collective-permute-done | bytes 524320 | tf_op jit(solution)/shard_map/ppermute | solution.py:249
  347.5 21.0 %collective-permute-done.8 = f32[1,1,512,256]{3,2,1,0:T(8,128)S(1)} collective-permute-done((f32[1,1,512,256]{3,2,1,0:T(8,128)S(1)}, f32[1,1,512,256]{3,2,1,0:T(8,128)S(1)}, u32[]{:S(2)}, u32[]{:S(2)}) %collective-permute-start.8) | collective-permute-done | bytes 524320 | tf_op jit(solution)/shard_map/ppermute | solution.py:249
  371.1 7.3 collective-permute-done.20
  378.6 6.6 collective-permute-done.22
  388.7 5.9 collective-permute-start.52
  397.0 11.3 %collective-permute-start.82 = (f32[64,2048]{1,0:T(8,128)S(1)}, f32[64,2048]{1,0:T(8,128)S(1)}, u32[]{:S(2)}, u32[]{:S(2)}) collective-permute-start(f32[64,2048]{1,0:T(8,128)S(1)} %constant_dynamic-slice_fusion.7), channel_id=1, source_target_pairs={{0,2},{1,3},{2,0},{3,1},{4,6},{5,7},{6,4},{7,5},{8,10},{9,11},{10,... | collective-permute-start | bytes 1572872 | tf_op jit(solution)/shard_map/ppermute | solution.py:249
  413.2 18.9 %collective-permute-done.53 = f32[64,1536]{1,0:T(8,128)S(1)} collective-permute-done((f32[64,1536]{1,0:T(8,128)S(1)}, f32[64,1536]{1,0:T(8,128)S(1)}, u32[]{:S(2)}, u32[]{:S(2)}) %collective-permute-start.53) | collective-permute-done | bytes 393248 | tf_op jit(solution)/shard_map/ppermute | solution.py:249
  434.7 9.0 %collective-permute-done.24 = f32[64,1536]{1,0:T(8,128)S(1)} collective-permute-done((f32[64,1536]{1,0:T(8,128)S(1)}, f32[64,1536]{1,0:T(8,128)S(1)}, u32[]{:S(2)}, u32[]{:S(2)}) %collective-permute-start.24) | collective-permute-done | bytes 393248 | tf_op jit(solution)/shard_map/ppermute | solution.py:249
  444.4 9.5 %collective-permute-done.61 = f32[64,1536]{1,0:T(8,128)S(1)} collective-permute-done((f32[64,1536]{1,0:T(8,128)S(1)}, f32[64,1536]{1,0:T(8,128)S(1)}, u32[]{:S(2)}, u32[]{:S(2)}) %collective-permute-start.61) | collective-permute-done | bytes 393248 | tf_op jit(solution)/shard_map/ppermute | solution.py:249
  454.7 8.6 %collective-permute-done.32 = f32[64,1536]{1,0:T(8,128)S(1)} collective-permute-done((f32[64,1536]{1,0:T(8,128)S(1)}, f32[64,1536]{1,0:T(8,128)S(1)}, u32[]{:S(2)}, u32[]{:S(2)}) %collective-permute-start.32) | collective-permute-done | bytes 393248 | tf_op jit(solution)/shard_map/ppermute | solution.py:249
  495.9 6.5 collective-permute-start.56
  567.0 5.9 collective-permute-done.93
  604.1 7.7 collective-permute-done.96
  634.5 32.1 %collective-permute-done.99 = bf16[512,512]{1,0:T(8,128)(2,1)S(1)} collective-permute-done((bf16[512,512]{1,0:T(8,128)(2,1)S(1)}, bf16[512,512]{1,0:T(8,128)(2,1)S(1)}, u32[]{:S(2)}, u32[]{:S(2)}) %collective-permute-start.99) | collective-permute-done | bytes 524320 | tf_op jit(solution)/shard_map/ppermute | solution.py:346
  666.6 11.0 %collective-permute-done.100 = bf16[512,512]{1,0:T(8,128)(2,1)S(1)} collective-permute-done((bf16[512,512]{1,0:T(8,128)(2,1)S(1)}, bf16[512,512]{1,0:T(8,128)(2,1)S(1)}, u32[]{:S(2)}, u32[]{:S(2)}) %collective-permute-start.100) | collective-permute-done | bytes 524320 | tf_op jit(solution)/shard_map/ppermute | solution.py:346
  686.4 155.8 %shard_map.50 = (bf16[512,2048]{1,0:T(8,128)(2,1)}, f32[512,2048]{1,0:T(8,128)}) custom-call(f32[512,1536]{1,0:T(8,128)} %pad_maximum_fusion.1.refs_0_, f32[512,1536]{1,0:T(8,128)} %pad_maximum_fusion.2.refs_1_, f32[512,2048]{1,0:T(8,128)} %pad_maximum_fusion.refs_2_, bf16[512,2048]{1,0:T(8,128)(2,1)} %pad_maximum_fusion.4.refs_3_, f32[512,2048]{1,0:T(8,128)} %refs_4_.1), custom_call_target="tpu_custom_call" | custom-call | flops 40000000000 | bytes 25165824 | tf_op jit(solution)/shard_map/pallas_call | solution.py:208
  (404 shorter events, 303.6 us)
Async XLA Ops:
  21.6 49.2 %collective-permute-start.42 = (bf16[512,512]{1,0:T(8,128)(2,1)}, bf16[512,512]{1,0:T(8,128)(2,1)}, u32[]{:S(2)}, u32[]{:S(2)}) collective-permute-start(bf16[512,512]{1,0:T(8,128)(2,1)} %get-tuple-element.22), channel_id=1, source_target_pairs={{8,0},{16,8},{24,16},{9,1},{17,9},{25,17},{10,2},{18,10},{26,18},{... | collective-permute-start | bytes 1572872 | tf_op jit(solution)/shard_map/ppermute | solution.py:276
  22.9 49.2 %collective-permute-start.41 = (bf16[512,512]{1,0:T(8,128)(2,1)}, bf16[512,512]{1,0:T(8,128)(2,1)}, u32[]{:S(2)}, u32[]{:S(2)}) collective-permute-start(bf16[512,512]{1,0:T(8,128)(2,1)} %get-tuple-element.22), channel_id=1, source_target_pairs={{0,8},{8,16},{16,24},{1,9},{9,17},{17,25},{2,10},{10,18},{18,26},{... | collective-permute-start | bytes 1572872 | tf_op jit(solution)/shard_map/ppermute | solution.py:273
  32.5 44.2 %collective-permute-start.1 = (bf16[512,512]{1,0:T(8,128)(2,1)S(1)}, bf16[512,512]{1,0:T(8,128)(2,1)}, u32[]{:S(2)}, u32[]{:S(2)}) collective-permute-start(bf16[512,512]{1,0:T(8,128)(2,1)S(1)} %get-tuple-element.21), channel_id=1, source_target_pairs={{8,0},{16,8},{24,16},{9,1},{17,9},{25,17},{10,2},{18,10},{26,18},{... | collective-permute-start | bytes 1572872 | tf_op jit(solution)/shard_map/ppermute | solution.py:276
  82.4 47.4 %collective-permute-start.2 = (bf16[512,512]{1,0:T(8,128)(2,1)}, bf16[512,512]{1,0:T(8,128)(2,1)S(1)}, u32[]{:S(2)}, u32[]{:S(2)}) collective-permute-start(bf16[512,512]{1,0:T(8,128)(2,1)} %collective-permute-done.1), channel_id=1, source_target_pairs={{8,0},{16,8},{9,1},{17,9},{10,2},{18,10},{11,3},{19,11},{12,4},{20... | collective-permute-start | bytes 1572872 | tf_op jit(solution)/shard_map/ppermute | solution.py:276
  87.5 42.9 %collective-permute-start.4 = (bf16[512,512]{1,0:T(8,128)(2,1)S(1)}, bf16[512,512]{1,0:T(8,128)(2,1)}, u32[]{:S(2)}, u32[]{:S(2)}) collective-permute-start(bf16[512,512]{1,0:T(8,128)(2,1)S(1)} %collective-permute-done), channel_id=1, source_target_pairs={{8,16},{16,24},{9,17},{17,25},{10,18},{18,26},{11,19},{19,27},{12,... | collective-permute-start | bytes 1572872 | tf_op jit(solution)/shard_map/ppermute | solution.py:273
  89.5 42.3 %collective-permute-start.14 = (bf16[512,512]{1,0:T(8,128)(2,1)S(1)}, bf16[512,512]{1,0:T(8,128)(2,1)S(1)}, u32[]{:S(2)}, u32[]{:S(2)}) collective-permute-start(bf16[512,512]{1,0:T(8,128)(2,1)S(1)} %collective-permute-done.13), channel_id=1, source_target_pairs={{8,0},{16,8},{9,1},{17,9},{10,2},{18,10},{11,3},{19,11},{12,4},{20... | collective-permute-start | bytes 1572872 | tf_op jit(solution)/shard_map/ppermute | solution.py:276
  131.8 41.5 %collective-permute-start.5 = (bf16[512,512]{1,0:T(8,128)(2,1)}, bf16[512,512]{1,0:T(8,128)(2,1)}, u32[]{:S(2)}, u32[]{:S(2)}) collective-permute-start(bf16[512,512]{1,0:T(8,128)(2,1)} %collective-permute-done.4), channel_id=1, source_target_pairs={{16,24},{17,25},{18,26},{19,27},{20,28},{21,29},{22,30},{23,31}} | collective-permute-start | bytes 1572872 | tf_op jit(solution)/shard_map/ppermute | solution.py:273
  133.3 70.0 %collective-permute-start.15 = (bf16[512,512]{1,0:T(8,128)(2,1)S(1)}, bf16[512,512]{1,0:T(8,128)(2,1)}, u32[]{:S(2)}, u32[]{:S(2)}) collective-permute-start(bf16[512,512]{1,0:T(8,128)(2,1)S(1)} %collective-permute-done.14), channel_id=1, source_target_pairs={{8,0},{9,1},{10,2},{11,3},{12,4},{13,5},{14,6},{15,7}} | collective-permute-start | bytes 1572872 | tf_op jit(solution)/shard_map/ppermute | solution.py:276
  134.6 70.0 %collective-permute-start.17 = (bf16[512,512]{1,0:T(8,128)(2,1)S(1)}, bf16[512,512]{1,0:T(8,128)(2,1)}, u32[]{:S(2)}, u32[]{:S(2)}) collective-permute-start(bf16[512,512]{1,0:T(8,128)(2,1)S(1)} %collective-permute-done.16), channel_id=1, source_target_pairs={{16,24},{17,25},{18,26},{19,27},{20,28},{21,29},{22,30},{23,31}} | collective-permute-start | bytes 1572872 | tf_op jit(solution)/shard_map/ppermute | solution.py:273
  140.5 93.1 %collective-permute-start.76 = (f32[2,2,1,512,512]{4,3,1,0,2:T(8,128)}, f32[2,2,1,512,512]{4,3,1,0,2:T(8,128)}, u32[]{:S(2)}, u32[]{:S(2)}) collective-permute-start(f32[2,2,1,512,512]{4,3,1,0,2:T(8,128)} %dynamic-slice_bitcast_fusion), channel_id=1, source_target_pairs={{0,1},{1,0},{2,3},{3,2},{4,5},{5,4},{6,7},{7,6},{8,9},{9,8},{10,11... | collective-permute-start | bytes 12582920 | tf_op jit(solution)/shard_map/ppermute | solution.py:249
  171.4 70.4 %collective-permute-start.47 = (f32[2,2,1,512,512]{4,3,1,0,2:T(8,128)}, f32[2,2,1,512,512]{4,3,1,0,2:T(8,128)}, u32[]{:S(2)}, u32[]{:S(2)}) collective-permute-start(f32[2,2,1,512,512]{4,3,1,0,2:T(8,128)} %dynamic-slice_bitcast_fusion.1), channel_id=1, source_target_pairs={{0,1},{1,0},{2,3},{3,2},{4,5},{5,4},{6,7},{7,6},{8,9},{9,8},{10,11... | collective-permute-start | bytes 12582920 | tf_op jit(solution)/shard_map/ppermute | solution.py:249
  203.2 44.2 %collective-permute-start.6 = (f32[2,2,1,512,512]{4,3,1,0,2:T(8,128)}, f32[2,2,1,512,512]{4,3,1,0,2:T(8,128)}, u32[]{:S(2)}, u32[]{:S(2)}) collective-permute-start(f32[2,2,1,512,512]{4,3,1,0,2:T(8,128)} %dynamic-slice_bitcast_fusion.3), channel_id=1, source_target_pairs={{0,1},{1,0},{2,3},{3,2},{4,5},{5,4},{6,7},{7,6},{8,9},{9,8},{10,11... | collective-permute-start | bytes 12582920 | tf_op jit(solution)/shard_map/ppermute | solution.py:249
  241.2 50.2 %collective-permute-start.79 = (f32[1,2,512,256]{3,2,1,0:T(8,128)S(1)}, f32[1,2,512,256]{3,2,1,0:T(8,128)}, u32[]{:S(2)}, u32[]{:S(2)}) collective-permute-start(f32[1,2,512,256]{3,2,1,0:T(8,128)S(1)} %constant_dynamic-slice_fusion.9), channel_id=1, source_target_pairs={{0,4},{1,5},{2,6},{3,7},{4,0},{5,1},{6,2},{7,3},{8,12},{9,13},{10,... | collective-permute-start | bytes 3145736 | tf_op jit(solution)/shard_map/ppermute | solution.py:249
  246.7 41.8 %collective-permute-start.48 = (f32[2,1,512,256]{3,2,1,0:T(8,128)}, f32[2,1,512,256]{3,2,1,0:T(8,128)}, u32[]{:S(2)}, u32[]{:S(2)}) collective-permute-start(f32[2,1,512,256]{3,2,1,0:T(8,128)} %constant_dynamic-slice_fusion.23), channel_id=1, source_target_pairs={{0,2},{1,3},{2,0},{3,1},{4,6},{5,7},{6,4},{7,5},{8,10},{9,11},{10,... | collective-permute-start | bytes 3145736 | tf_op jit(solution)/shard_map/ppermute | solution.py:249
  247.5 46.1 %collective-permute-start.50 = (f32[1,2,512,256]{3,2,1,0:T(8,128)S(1)}, f32[1,2,512,256]{3,2,1,0:T(8,128)}, u32[]{:S(2)}, u32[]{:S(2)}) collective-permute-start(f32[1,2,512,256]{3,2,1,0:T(8,128)S(1)} %constant_dynamic-slice_fusion.21), channel_id=1, source_target_pairs={{0,4},{1,5},{2,6},{3,7},{4,0},{5,1},{6,2},{7,3},{8,12},{9,13},{10,... | collective-permute-start | bytes 3145736 | tf_op jit(solution)/shard_map/ppermute | solution.py:249
  253.2 57.6 %collective-permute-start.7 = (f32[2,1,512,256]{3,2,1,0:T(8,128)S(1)}, f32[2,1,512,256]{3,2,1,0:T(8,128)S(1)}, u32[]{:S(2)}, u32[]{:S(2)}) collective-permute-start(f32[2,1,512,256]{3,2,1,0:T(8,128)S(1)} %constant_dynamic-slice_fusion.39), channel_id=1, source_target_pairs={{0,2},{1,3},{2,0},{3,1},{4,6},{5,7},{6,4},{7,5},{8,10},{9,11},{10,... | collective-permute-start | bytes 3145736 | tf_op jit(solution)/shard_map/ppermute | solution.py:249
  266.0 46.5 %collective-permute-start.9 = (f32[1,2,512,256]{3,2,1,0:T(8,128)S(1)}, f32[1,2,512,256]{3,2,1,0:T(8,128)S(1)}, u32[]{:S(2)}, u32[]{:S(2)}) collective-permute-start(f32[1,2,512,256]{3,2,1,0:T(8,128)S(1)} %constant_dynamic-slice_fusion.37), channel_id=1, source_target_pairs={{0,4},{1,5},{2,6},{3,7},{4,0},{5,1},{6,2},{7,3},{8,12},{9,13},{10,... | collective-permute-start | bytes 3145736 | tf_op jit(solution)/shard_map/ppermute | solution.py:249
  288.5 44.8 %collective-permute-start.19 = (f32[2,1,512,256]{3,2,1,0:T(8,128)S(1)}, f32[2,1,512,256]{3,2,1,0:T(8,128)S(1)}, u32[]{:S(2)}, u32[]{:S(2)}) collective-permute-start(f32[2,1,512,256]{3,2,1,0:T(8,128)S(1)} %constant_dynamic-slice_fusion.35), channel_id=1, source_target_pairs={{0,2},{1,3},{2,0},{3,1},{4,6},{5,7},{6,4},{7,5},{8,10},{9,11},{10,... | collective-permute-start | bytes 3145736 | tf_op jit(solution)/shard_map/ppermute | solution.py:249
  291.5 43.6 %collective-permute-start.21 = (f32[1,2,512,256]{3,2,1,0:T(8,128)S(1)}, f32[1,2,512,256]{3,2,1,0:T(8,128)S(1)}, u32[]{:S(2)}, u32[]{:S(2)}) collective-permute-start(f32[1,2,512,256]{3,2,1,0:T(8,128)S(1)} %constant_dynamic-slice_fusion.33), channel_id=1, source_target_pairs={{0,4},{1,5},{2,6},{3,7},{4,0},{5,1},{6,2},{7,3},{8,12},{9,13},{10,... | collective-permute-start | bytes 3145736 | tf_op jit(solution)/shard_map/ppermute | solution.py:249
  293.6 52.5 %collective-permute-start.78 = (f32[1,1,512,256]{3,2,1,0:T(8,128)S(1)}, f32[1,1,512,256]{3,2,1,0:T(8,128)S(1)}, u32[]{:S(2)}, u32[]{:S(2)}) collective-permute-start(f32[1,1,512,256]{3,2,1,0:T(8,128)S(1)} %constant_dynamic-slice_fusion.10), channel_id=1, source_target_pairs={{0,4},{1,5},{2,6},{3,7},{4,0},{5,1},{6,2},{7,3},{8,12},{9,13},{10,... | collective-permute-start | bytes 1572872 | tf_op jit(solution)/shard_map/ppermute | solution.py:249
  312.5 72.7 %collective-permute-start.49 = (f32[1,1,512,256]{3,2,1,0:T(8,128)S(1)}, f32[1,1,512,256]{3,2,1,0:T(8,128)S(1)}, u32[]{:S(2)}, u32[]{:S(2)}) collective-permute-start(f32[1,1,512,256]{3,2,1,0:T(8,128)S(1)} %constant_dynamic-slice_fusion.22), channel_id=1, source_target_pairs={{0,4},{1,5},{2,6},{3,7},{4,0},{5,1},{6,2},{7,3},{8,12},{9,13},{10,... | collective-permute-start | bytes 1572872 | tf_op jit(solution)/shard_map/ppermute | solution.py:249
  333.3 52.6 %collective-permute-start.51 = (f32[1,1,512,256]{3,2,1,0:T(8,128)S(1)}, f32[1,1,512,256]{3,2,1,0:T(8,128)S(1)}, u32[]{:S(2)}, u32[]{:S(2)}) collective-permute-start(f32[1,1,512,256]{3,2,1,0:T(8,128)S(1)} %constant_dynamic-slice_fusion.20), channel_id=1, source_target_pairs={{0,2},{1,3},{2,0},{3,1},{4,6},{5,7},{6,4},{7,5},{8,10},{9,11},{10,... | collective-permute-start | bytes 1572872 | tf_op jit(solution)/shard_map/ppermute | solution.py:249
  369.1 258.5 %collective-permute-start.102 = (bf16[512,512]{1,0:T(8,128)(2,1)S(1)}, bf16[512,512]{1,0:T(8,128)(2,1)S(1)}, u32[]{:S(2)}, u32[]{:S(2)}) collective-permute-start(bf16[512,512]{1,0:T(8,128)(2,1)S(1)} %pad_maximum_fusion.14), channel_id=1, source_target_pairs={{0,0},{1,8},{2,16},{3,24},{4,1},{5,9},{6,17},{7,25},{8,2},{9,10},{... | collective-permute-start | bytes 1572872 | tf_op jit(solution)/shard_map/ppermute | solution.py:346
  386.1 248.3 %collective-permute-start.101 = (bf16[512,512]{1,0:T(8,128)(2,1)S(1)}, bf16[512,512]{1,0:T(8,128)(2,1)S(1)}, u32[]{:S(2)}, u32[]{:S(2)}) collective-permute-start(bf16[512,512]{1,0:T(8,128)(2,1)S(1)} %pad_maximum_fusion.13), channel_id=1, source_target_pairs={{0,0},{1,8},{2,16},{3,24},{4,1},{5,9},{6,17},{7,25},{8,2},{9,10},{... | collective-permute-start | bytes 1572872 | tf_op jit(solution)/shard_map/ppermute | solution.py:346
  397.0 67.1 %collective-permute-start.82 = (f32[64,2048]{1,0:T(8,128)S(1)}, f32[64,2048]{1,0:T(8,128)S(1)}, u32[]{:S(2)}, u32[]{:S(2)}) collective-permute-start(f32[64,2048]{1,0:T(8,128)S(1)} %constant_dynamic-slice_fusion.7), channel_id=1, source_target_pairs={{0,2},{1,3},{2,0},{3,1},{4,6},{5,7},{6,4},{7,5},{8,10},{9,11},{10,... | collective-permute-start | bytes 1572872 | tf_op jit(solution)/shard_map/ppermute | solution.py:249
  408.4 57.3 %collective-permute-start.90 = (f32[64,2048]{1,0:T(8,128)S(1)}, f32[64,2048]{1,0:T(8,128)S(1)}, u32[]{:S(2)}, u32[]{:S(2)}) collective-permute-start(f32[64,2048]{1,0:T(8,128)S(1)} %constant_dynamic-slice_fusion.3), channel_id=1, source_target_pairs={{0,4},{1,5},{2,6},{3,7},{4,0},{5,1},{6,2},{7,3},{8,12},{9,13},{10,... | collective-permute-start | bytes 1572872 | tf_op jit(solution)/shard_map/ppermute | solution.py:249
  472.0 50.9 %collective-permute-start.83 = (f32[32,2048]{1,0:T(8,128)S(1)}, f32[32,2048]{1,0:T(8,128)S(1)}, u32[]{:S(2)}, u32[]{:S(2)}) collective-permute-start(f32[32,2048]{1,0:T(8,128)S(1)} %constant_dynamic-slice_fusion.6), channel_id=1, source_target_pairs={{0,4},{1,5},{2,6},{3,7},{4,0},{5,1},{6,2},{7,3},{8,12},{9,13},{10,... | collective-permute-start | bytes 786440 | tf_op jit(solution)/shard_map/ppermute | solution.py:249
  474.5 52.8 %collective-permute-start.91 = (f32[32,2048]{1,0:T(8,128)S(1)}, f32[32,2048]{1,0:T(8,128)S(1)}, u32[]{:S(2)}, u32[]{:S(2)}) collective-permute-start(f32[32,2048]{1,0:T(8,128)S(1)} %constant_dynamic-slice_fusion.2), channel_id=1, source_target_pairs={{0,2},{1,3},{2,0},{3,1},{4,6},{5,7},{6,4},{7,5},{8,10},{9,11},{10,... | collective-permute-start | bytes 786440 | tf_op jit(solution)/shard_map/ppermute | solution.py:249
  621.5 57.7 %collective-permute-start.69 = (f32[256,1536]{1,0:T(8,128)S(1)}, f32[256,1536]{1,0:T(8,128)S(1)}, u32[]{:S(2)}, u32[]{:S(2)}) collective-permute-start(f32[256,1536]{1,0:T(8,128)S(1)} %pad_maximum_fusion.6), channel_id=1, source_target_pairs={{0,1},{1,0},{2,3},{3,2},{4,5},{5,4},{6,7},{7,6},{8,9},{9,8},{10,11... | collective-permute-start | bytes 4718600 | tf_op jit(solution)/shard_map/ppermute | solution.py:249
  627.7 49.9 %collective-permute-start.100 = (bf16[512,512]{1,0:T(8,128)(2,1)S(1)}, bf16[512,512]{1,0:T(8,128)(2,1)S(1)}, u32[]{:S(2)}, u32[]{:S(2)}) collective-permute-start(bf16[512,512]{1,0:T(8,128)(2,1)S(1)} %pad_maximum_fusion.12), channel_id=1, source_target_pairs={{0,0},{1,8},{2,16},{3,24},{4,1},{5,9},{6,17},{7,25},{8,2},{9,10},{... | collective-permute-start | bytes 1572872 | tf_op jit(solution)/shard_map/ppermute | solution.py:346
  632.6 48.7 %collective-permute-start.40 = (f32[256,1536]{1,0:T(8,128)S(1)}, f32[256,1536]{1,0:T(8,128)S(1)}, u32[]{:S(2)}, u32[]{:S(2)}) collective-permute-start(f32[256,1536]{1,0:T(8,128)S(1)} %pad_maximum_fusion.5), channel_id=1, source_target_pairs={{0,1},{1,0},{2,3},{3,2},{4,5},{5,4},{6,7},{7,6},{8,9},{9,8},{10,11... | collective-permute-start | bytes 4718600 | tf_op jit(solution)/shard_map/ppermute | solution.py:249
  634.4 49.1 %collective-permute-start.98 = (f32[256,2048]{1,0:T(8,128)S(1)}, f32[256,2048]{1,0:T(8,128)S(1)}, u32[]{:S(2)}, u32[]{:S(2)}) collective-permute-start(f32[256,2048]{1,0:T(8,128)S(1)} %pad_maximum_fusion.3), channel_id=1, source_target_pairs={{0,1},{1,0},{2,3},{3,2},{4,5},{5,4},{6,7},{7,6},{8,9},{9,8},{10,11... | collective-permute-start | bytes 6291464 | tf_op jit(solution)/shard_map/ppermute | solution.py:249
  (86 other events, 1278.8 us)
